TPU v7x, 256 devices: a whole 4x4x8 slice. The times are simulated.
256 devices in a mesh: sec: 8 (over x, y_lo), ctx: 32 (over z, y_hi, core).
Axes of the slice: x: 4, y: 4 (y_hi: 2, y_lo: 2; y = y_hi * 2 + y_lo), z: 8, core: 2. Of those that a mesh axis runs over, the one named last changes fastest.
Arguments:
- hidden_state: bfloat16 [8, 4096, 4096], P('sec', 'ctx'), may hold values from -8 to 8
- queries: bfloat16 [8, 4096, 4096], P('sec', 'ctx'), may hold values from -6 to 6
- key_vectors: bfloat16 [8, 4096, 4096], P('sec', 'ctx'), may hold values from -4.5 to 4.5
- value_vectors: bfloat16 [8, 4096, 4096], P('sec', 'ctx'), may hold values from -6 to 6
- modulation: float32 [32, 3, 4096], replicated, may hold values from -3 to 3
- down_weight: bfloat16 [4096, 256], replicated, may hold values from -0.09375 to 0.09375
- conv_weight: bfloat16 [3, 3, 3, 256, 256], replicated, may hold values from -0.078125 to 0.078125
- clip_frames: int32 [8], replicated, may hold values from 16 to 64, as said below
- destination: int32 [8], replicated, may hold values from 0 to 7, as said below
- timestep: int32 [8], replicated, may hold values from 0 to 31
Outputs:
- upsampled: bfloat16 [8, 4096, 256], P('sec', 'ctx')
Inputs may be any that keep to these rules, and one draw needn't show every extreme that they name: `clip_frames`: one section's clip fills all 64 frames. `destination`: every upsampler group receives exactly one clip; some group d receives the clip of section (d + 4) mod 8.
All inputs are finite; a program needn't handle non-finite values.
Results may differ from a plain program's by a relative error of at most 0.0063.
Values may be sent and summed in bfloat16 or wider, within the bound.
A program may use at most 64 MiB of HBM per device.

v0:
```python
import math
import jax
import jax.numpy as jnp
from jax import lax
from jax.sharding import PartitionSpec as P

HEADS = 32
HH = 8
WW = 8


def extended(block, sides, width):
    for axis, dim in sides:
        count = lax.axis_size(axis)
        forward = [(i, i + 1) for i in range(count - 1)]
        backward = [(target, source) for source, target in forward]
        low = lax.ppermute(
            lax.slice_in_dim(block, block.shape[dim] - width, None, axis=dim), axis, forward
        )
        high = lax.ppermute(lax.slice_in_dim(block, 0, width, axis=dim), axis, backward)
        block = jnp.concatenate([low, block, high], axis=dim)
    return block


def attend_heads(tensors, frames):
    query_part, key_part, value_part = tensors
    item_count, seq_len, local_heads, head_size = query_part.shape
    block_rows = min(512, seq_len)
    score_scale = 1.0 / math.sqrt(head_size)
    positions = jnp.arange(seq_len, dtype=jnp.int32) // (HH * WW)
    key_valid = positions < frames
    query_blocks = query_part.reshape(
        item_count, seq_len // block_rows, block_rows, local_heads, head_size
    )
    query_blocks = jnp.moveaxis(query_blocks, 1, 0)

    def one_block(query_block):
        scores = (
            jnp.einsum("nqhd,nkhd->nhqk", query_block, key_part, preferred_element_type=jnp.float32)
            * score_scale
        )
        scores = jnp.where(key_valid[None, None, None, :], scores, -jnp.inf)
        weights = jnp.exp(scores - jnp.max(scores, axis=3, keepdims=True))
        row_total = jnp.sum(weights, axis=3)
        rounded = weights.astype(jnp.bfloat16)
        product = jnp.einsum(
            "nhqk,nkhd->nqhd", rounded, value_part, preferred_element_type=jnp.float32
        )
        return (product / jnp.moveaxis(row_total, 1, 2)[..., None]).astype(jnp.bfloat16)

    result = lax.map(one_block, query_blocks)
    return jnp.moveaxis(result, 0, 1).reshape(item_count, seq_len, local_heads, head_size)


def adapt_input(block_out, mod_rows, down_weight):
    wide_values = block_out.astype(jnp.float32)
    centre = jnp.mean(wide_values, axis=-1, keepdims=True)
    spread = jnp.mean(jnp.square(wide_values - centre), axis=-1, keepdims=True)
    normed = (
        (wide_values - centre) * lax.rsqrt(spread + 1e-06) * (1.0 + mod_rows[1]) + mod_rows[0]
    ).astype(jnp.bfloat16)
    return jnp.einsum(
        "std,dc->stc", normed, down_weight, preferred_element_type=jnp.float32
    ).astype(jnp.bfloat16)


def body(
    hidden_state,
    queries,
    key_vectors,
    value_vectors,
    modulation,
    down_weight,
    conv_weight,
    clip_frames,
    destination,
    timestep,
):
    my_section = lax.axis_index("sec")
    my_place = lax.axis_index("ctx")
    sections, tok_rows, model_width = hidden_state.shape
    head_size = model_width // HEADS
    own_frames = clip_frames[my_section]
    my_step = timestep[my_section]

    def by_heads(tensor):
        return tensor.reshape(sections, tok_rows, HEADS, head_size)

    local_out = attend_heads(
        (
            lax.all_to_all(by_heads(queries), "ctx", split_axis=2, concat_axis=1, tiled=True),
            lax.all_to_all(by_heads(key_vectors), "ctx", split_axis=2, concat_axis=1, tiled=True),
            lax.all_to_all(by_heads(value_vectors), "ctx", split_axis=2, concat_axis=1, tiled=True),
        ),
        own_frames,
    )
    attended = lax.all_to_all(local_out, "ctx", split_axis=1, concat_axis=2, tiled=True)
    attended = attended.reshape(sections, tok_rows, model_width)
    block_out = (
        hidden_state.astype(jnp.float32) + modulation[my_step, 2] * attended.astype(jnp.float32)
    ).astype(jnp.bfloat16)
    section_ids = jnp.arange(destination.shape[0], dtype=jnp.int32)
    source = jnp.sum(jnp.where(destination == my_section, section_ids, 0))
    own_projected = adapt_input(block_out, modulation[my_step], down_weight)
    gathered = lax.all_gather(own_projected, "sec", axis=0, tiled=True)
    first_row = jnp.int32(0)
    piece_rows = gathered.shape[0]
    offset = jnp.clip(source, 0, piece_rows - 1)
    chosen = lax.dynamic_index_in_dim(gathered, offset, 0, keepdims=True)
    inside = (source >= first_row) & (source < first_row + piece_rows)
    projected = jnp.where(inside, chosen, jnp.zeros_like(own_projected))
    frames_here = tok_rows // (HH * WW)
    frame_number = my_place * frames_here + jnp.arange(frames_here, dtype=jnp.int32)
    keep_frame = (frame_number < clip_frames[source])[None, :, None, None, None]
    clip_cells = jnp.where(keep_frame, projected.reshape(sections, frames_here, HH, WW, -1), 0)
    padded = extended(clip_cells, (("ctx", 1),), 1)
    convolved = lax.conv_general_dilated(
        padded,
        conv_weight,
        (1, 1, 1),
        ((0, 0), (1, 1), (1, 1)),
        dimension_numbers=("NDHWC", "DHWIO", "NDHWC"),
        preferred_element_type=jnp.float32,
    )
    upsampled = jnp.where(keep_frame, clip_cells.astype(jnp.float32) + convolved, 0.0).astype(
        jnp.bfloat16
    )
    return upsampled.reshape(sections, tok_rows, -1)


def solution(mesh):
    in_specs = (
        P("sec", "ctx", None),
        P("sec", "ctx", None),
        P("sec", "ctx", None),
        P("sec", "ctx", None),
        P(),
        P(),
        P(),
        P(),
        P(),
        P(),
    )
    out_specs = P("sec", "ctx", None)
    return jax.shard_map(body, mesh=mesh, in_specs=in_specs, out_specs=out_specs, check_vma=False)
```

profile of v0, /device:TPU:1, one launch (start us, length us, event | category | flops | bytes accessed | tf_op | source)
XLA Modules:
  0.0 303.9 jit_solution(16420890058449033828)
XLA Ops:
  2.4 12.8 %all-to-all-start = ((bf16[1,128,32,128]{1,3,0,2:T(8,128)(2,1)}), bf16[1,128,32,128]{1,3,0,2:T(8,128)(2,1)}, u32[]{:S(2)}, u32[]{:S(2)}) async-start(bf16[1,128,32,128]{1,3,0,2:T(8,128)(2,1)} %bitcast.99), calls=%async_computation | async-start | bytes 2097152 | tf_op jit(solution)/shard_map/all_to_all | solution.py:91
  17.5 25.9 %all-to-all-done = bf16[1,128,32,128]{1,3,0,2:T(8,128)(2,1)} async-done(((bf16[1,128,32,128]{1,3,0,2:T(8,128)(2,1)}), bf16[1,128,32,128]{1,3,0,2:T(8,128)(2,1)}, u32[]{:S(2)}, u32[]{:S(2)}) %all-to-all-start) | async-done | bytes 1048608 | tf_op jit(solution)/shard_map/all_to_all | solution.py:91
  43.4 5.8 %all-to-all-start.1 = ((bf16[1,128,32,128]{1,3,0,2:T(8,128)(2,1)}), bf16[1,128,32,128]{1,3,0,2:T(8,128)(2,1)}, u32[]{:S(2)}, u32[]{:S(2)}) async-start(bf16[1,128,32,128]{1,3,0,2:T(8,128)(2,1)} %bitcast.98), calls=%async_computation.1 | async-start | bytes 2097152 | tf_op jit(solution)/shard_map/all_to_all | solution.py:92
  51.6 25.9 %all-to-all-done.1 = bf16[1,128,32,128]{1,3,0,2:T(8,128)(2,1)} async-done(((bf16[1,128,32,128]{1,3,0,2:T(8,128)(2,1)}), bf16[1,128,32,128]{1,3,0,2:T(8,128)(2,1)}, u32[]{:S(2)}, u32[]{:S(2)}) %all-to-all-start.1) | async-done | bytes 1048608 | tf_op jit(solution)/shard_map/all_to_all | solution.py:92
  77.5 5.9 %all-to-all-start.2 = ((bf16[1,128,32,128]{1,3,0,2:T(8,128)(2,1)}), bf16[1,128,32,128]{1,3,0,2:T(8,128)(2,1)}, u32[]{:S(2)}, u32[]{:S(2)}) async-start(bf16[1,128,32,128]{1,3,0,2:T(8,128)(2,1)} %bitcast.97), calls=%async_computation.2 | async-start | bytes 2097152 | tf_op jit(solution)/shard_map/all_to_all | solution.py:93
  91.1 20.4 %all-to-all-done.2 = bf16[1,128,32,128]{1,3,0,2:T(8,128)(2,1)} async-done(((bf16[1,128,32,128]{1,3,0,2:T(8,128)(2,1)}), bf16[1,128,32,128]{1,3,0,2:T(8,128)(2,1)}, u32[]{:S(2)}, u32[]{:S(2)}) %all-to-all-start.2) | async-done | bytes 1048608 | tf_op jit(solution)/shard_map/all_to_all | solution.py:93
  113.8 63.7 %while.11 = (s32[]{:T(128)}, bf16[8,1,512,1,128]{4,2,3,1,0:T(8,128)(2,1)}, bf16[8,1,512,1,128]{4,2,3,1,0:T(8,128)(2,1)}, bf16[1,4096,1,128]{3,1,2,0:T(8,128)(2,1...) while((s32[]{:T(128)}, bf16[8,1,512,1,128]{4,2,3,1,0:T(8,128)(2,1)}, ...), condition=%wide.region_4.5_spmd.clone, body=%wide.region_1.4_spmd.clone.sunk | while | flops 1096977408 | bytes 31746172 | solution.py:51
  114.4 2.7 fusion.69
  122.4 2.7 fusion.69
  130.4 2.7 fusion.69
  146.3 2.7 fusion.69
  154.2 2.7 fusion.69
  162.2 2.7 fusion.69
  170.2 2.7 fusion.69
  177.5 4.3 %copy.55 = bf16[1,4096,1,128]{3,2,0,1:T(2,128)(2,1)} copy(bf16[1,4096,1,128]{3,1,2,0:T(8,128)(2,1)} %bitcast.101) | data formatting | bytes 2097152 | tf_op jit(solution)/shard_map/reshape;transpose | solution.py:52
  182.3 24.3 %reduce.6 = bf16[4096,128]{1,0:T(8,128)(2,1)} reduce(bf16[4096,1,1,128]{3,2,1,0:T(2,128)(2,1)} %bitcast.95, bf16[]{:T(256)} %broadcast.118), dimensions={1,2}, to_apply=%bitcast.83.reduce_sub_computation | reduce | bytes 2097154
  208.8 5.9 %all-to-all-start.3 = ((bf16[32,2,8192]{2,1,0:T(2,128)(2,1)}), bf16[32,2,8192]{2,1,0:T(2,128)(2,1)}, u32[]{:S(2)}, u32[]{:S(2)}) async-start(bf16[32,2,8192]{2,1,0:T(2,128)(2,1)} %reshape.170), calls=%async_computation.3 | async-start | bytes 2097152 | tf_op jit(solution)/shard_map/all_to_all | solution.py:97
  221.9 20.8 %all-to-all-done.3 = bf16[32,2,8192]{2,1,0:T(2,128)(2,1)} async-done(((bf16[32,2,8192]{2,1,0:T(2,128)(2,1)}), bf16[32,2,8192]{2,1,0:T(2,128)(2,1)}, u32[]{:S(2)}, u32[]{:S(2)}) %all-to-all-start.3) | async-done | bytes 1048608 | tf_op jit(solution)/shard_map/all_to_all | solution.py:97
  242.7 5.8 %reshape.171 = bf16[4096,1,1,128]{3,2,1,0:T(2,128)(2,1)} reshape(bf16[32,2,8192]{2,1,0:T(2,128)(2,1)} %all-to-all-done.3) | data formatting | bytes 2097152
  248.4 3.8 %bitcast_convert_fusion = f32[1,4096,1,128]{3,2,0,1:T(1,128)S(1)} fusion(bf16[4096,1,1,128]{3,2,1,0:T(2,128)(2,1)} %reshape.171), kind=kLoop, calls=%fused_computation.65 | loop fusion | flops 524288 | bytes 3145728 | tf_op jit(solution)/shard_map/convert_element_type | solution.py:100
  261.0 23.3 %all-gather = bf16[1024,256]{1,0:T(8,128)(2,1)S(1)} all-gather(bf16[128,256]{1,0:T(8,128)(2,1)S(1)} %convolution_convert_fusion), channel_id=2, replica_groups=mesh['sec'=8,'ctx'=32] {'sec'}, dimensions={0}, use_global_device_ids=true | all-gather | bytes 589824 | tf_op jit(solution)/shard_map/all_gather | solution.py:105
  284.6 9.2 %collective-permute-start.1 = (bf16[1,1,8,8,256]{4,0,3,2,1:T(2,128)(2,1)S(1)}, bf16[1,1,8,8,256]{4,0,3,2,1:T(2,128)(2,1)S(1)}, u32[]{:S(2)}, u32[]{:S(2)}) collective-permute-start(bf16[1,1,8,8,256]{4,0,3,2,1:T(2,128)(2,1)S(1)} %get-tuple-element.97), channel_id=1, source_target_pairs={{1,0},{2,1},{3,2},{4,3},{5,4},{6,5},{7,6},{8,7},{9,8},{10,9},{11,1... | collective-permute-start | bytes 98312 | tf_op jit(solution)/shard_map/ppermute | solution.py:20
  293.8 4.8 %collective-permute-start = (bf16[1,1,8,8,256]{4,0,3,2,1:T(2,128)(2,1)S(1)}, bf16[1,1,8,8,256]{4,0,3,2,1:T(2,128)(2,1)S(1)}, u32[]{:S(2)}, u32[]{:S(2)}) collective-permute-start(bf16[1,1,8,8,256]{4,0,3,2,1:T(2,128)(2,1)S(1)} %get-tuple-element.96), channel_id=1, source_target_pairs={{0,1},{1,2},{2,3},{3,4},{4,5},{5,6},{6,7},{7,8},{8,9},{9,10},{10,1... | collective-permute-start | bytes 98312 | tf_op jit(solution)/shard_map/ppermute | solution.py:17
  300.0 3.2 %fusion.42 = bf16[1,2,8,8,256]{4,0,3,2,1:T(2,128)(2,1)S(1)} fusion(bf16[3,3,3,256,256]{4,3,2,1,0:T(8,128)(2,1)S(1)} %copy-done, bf16[1,1,8,8,256]{4,0,3,2,1:T(2,128)(2,1)S(1)} %collective-permute-done.1, bf16[1,2,8,8,256]{4,0,3,2,1:T(2,128)(2,1)S(1)} %broadcast_select_fusion, bf16[1,1,8,8,256]{4,0,3,2,1:T(2,128)(2,1)S(1)} %collective-permute-done, ...), kind=kOutput, calls=%fused_computation.40 | convolution fusion | flops 381157376 | bytes 3735554 | tf_op jit(solution)/shard_map/conv_general_dilated | solution.py:117
  (84 shorter events, 76.4 us)
Async XLA Ops:
  0.0 300.0 %copy-start = (bf16[3,3,3,256,256]{4,3,2,1,0:T(8,128)(2,1)S(1)}, bf16[3,3,3,256,256]{4,3,2,1,0:T(8,128)(2,1)}, u32[]{:S(2)}) copy-start(bf16[3,3,3,256,256]{4,3,2,1,0:T(8,128)(2,1)} %param.18) | copy-start | bytes 10616836
  2.4 41.0 %all-to-all-start = ((bf16[1,128,32,128]{1,3,0,2:T(8,128)(2,1)}), bf16[1,128,32,128]{1,3,0,2:T(8,128)(2,1)}, u32[]{:S(2)}, u32[]{:S(2)}) async-start(bf16[1,128,32,128]{1,3,0,2:T(8,128)(2,1)} %bitcast.99), calls=%async_computation | async-start | bytes 2097152 | tf_op jit(solution)/shard_map/all_to_all | solution.py:91
  43.4 34.0 %all-to-all-start.1 = ((bf16[1,128,32,128]{1,3,0,2:T(8,128)(2,1)}), bf16[1,128,32,128]{1,3,0,2:T(8,128)(2,1)}, u32[]{:S(2)}, u32[]{:S(2)}) async-start(bf16[1,128,32,128]{1,3,0,2:T(8,128)(2,1)} %bitcast.98), calls=%async_computation.1 | async-start | bytes 2097152 | tf_op jit(solution)/shard_map/all_to_all | solution.py:92
  49.3 34.0 %copy-start.7 = (s32[8]{0:T(128)S(1)}, s32[8]{0:T(128)}, u32[]{:S(2)}) copy-start(s32[8]{0:T(128)} %param.20) | copy-start | bytes 100
  49.3 36.6 %copy-start.4 = (s32[8]{0:T(128)S(1)}, s32[8]{0:T(128)}, u32[]{:S(2)}) copy-start(s32[8]{0:T(128)} %param.19) | copy-start | bytes 100
  77.5 34.0 %all-to-all-start.2 = ((bf16[1,128,32,128]{1,3,0,2:T(8,128)(2,1)}), bf16[1,128,32,128]{1,3,0,2:T(8,128)(2,1)}, u32[]{:S(2)}, u32[]{:S(2)}) async-start(bf16[1,128,32,128]{1,3,0,2:T(8,128)(2,1)} %bitcast.97), calls=%async_computation.2 | async-start | bytes 2097152 | tf_op jit(solution)/shard_map/all_to_all | solution.py:93
  117.2 2.2 copy-start.1
  125.1 2.2 copy-start.1
  133.1 2.2 copy-start.1
  141.1 2.2 copy-start.1
  149.0 2.2 copy-start.1
  157.0 2.2 copy-start.1
  164.9 2.2 copy-start.1
  172.9 2.2 copy-start.1
  206.7 10.0 %copy-start.8 = (s32[8]{0:T(128)S(1)}, s32[8]{0:T(128)}, u32[]{:S(2)}) copy-start(s32[8]{0:T(128)} %param.21) | copy-start | bytes 100
  208.8 33.9 %all-to-all-start.3 = ((bf16[32,2,8192]{2,1,0:T(2,128)(2,1)}), bf16[32,2,8192]{2,1,0:T(2,128)(2,1)}, u32[]{:S(2)}, u32[]{:S(2)}) async-start(bf16[32,2,8192]{2,1,0:T(2,128)(2,1)} %reshape.170), calls=%async_computation.3 | async-start | bytes 2097152 | tf_op jit(solution)/shard_map/all_to_all | solution.py:97
  257.5 2.9 copy-start.2
  257.5 2.9 copy-start.3
  257.5 2.9 copy-start.6
  260.4 23.9 %copy-start.5 = (pred[2]{0:T(512)(128)(4,1)S(1)}, pred[2]{0:T(512)(128)(4,1)}, u32[]{:S(2)}) copy-start(pred[2]{0:T(512)(128)(4,1)} %add_compare_fusion) | copy-start | bytes 10
  284.6 14.0 %collective-permute-start.1 = (bf16[1,1,8,8,256]{4,0,3,2,1:T(2,128)(2,1)S(1)}, bf16[1,1,8,8,256]{4,0,3,2,1:T(2,128)(2,1)S(1)}, u32[]{:S(2)}, u32[]{:S(2)}) collective-permute-start(bf16[1,1,8,8,256]{4,0,3,2,1:T(2,128)(2,1)S(1)} %get-tuple-element.97), channel_id=1, source_target_pairs={{1,0},{2,1},{3,2},{4,3},{5,4},{6,5},{7,6},{8,7},{9,8},{10,9},{11,1... | collective-permute-start | bytes 98312 | tf_op jit(solution)/shard_map/ppermute | solution.py:20
  293.8 6.2 %collective-permute-start = (bf16[1,1,8,8,256]{4,0,3,2,1:T(2,128)(2,1)S(1)}, bf16[1,1,8,8,256]{4,0,3,2,1:T(2,128)(2,1)S(1)}, u32[]{:S(2)}, u32[]{:S(2)}) collective-permute-start(bf16[1,1,8,8,256]{4,0,3,2,1:T(2,128)(2,1)S(1)} %get-tuple-element.96), channel_id=1, source_target_pairs={{0,1},{1,2},{2,3},{3,4},{4,5},{5,6},{6,7},{7,8},{8,9},{9,10},{10,1... | collective-permute-start | bytes 98312 | tf_op jit(solution)/shard_map/ppermute | solution.py:17
where the time goes:
time: 305 us; the launch traced here: 304 us
  waiting for transfers between devices  94.3 us (31%)
  other arithmetic  56.8 us (19%)
  matrix products  45.1 us (15%)
  starting transfers between devices  44.4 us (15%)
  local copies, waits for them, and re-layouts  33.8 us (11%)
  blocking collectives  23.3 us (8%)
  between operations  6.06 us (2%)
    all_to_all x1, waiting for transfers between devices, body(): lax.all_to_all(by_heads(queries), 'ctx', split_axis=2, concat_axis=1, til...  25.9 us
    all_to_all x1, waiting for transfers between devices, body(): lax.all_to_all(by_heads(key_vectors), 'ctx', split_axis=2, concat_axis=1,...  25.9 us
    unnamed x1, other arithmetic  24.3 us
    all_gather x1, blocking collectives, body(): gathered = lax.all_gather(own_projected, 'sec', axis=0, tiled=True)  23.3 us
    dot_general x8, matrix products, one_block(): jnp.einsum('nqhd,nkhd->nhqk', query_block, key_part, preferred_element_ty...  22 us
    all_to_all x1, waiting for transfers between devices, body(): lax.all_to_all(local_out, 'ctx', split_axis=1, concat_axis=2, tiled=True)  20.8 us
    all_to_all x1, waiting for transfers between devices, body(): lax.all_to_all(by_heads(value_vectors), 'ctx', split_axis=2, concat_axis=...  20.4 us
    dot_general x8, matrix products, one_block(): jnp.einsum('nhqk,nkhd->nqhd', rounded, value_part, preferred_element_type...  19.3 us
  transfers between devices with their start and end apart: 6, of which 5 were waited for; matrix products, arithmetic and copies ran while one was open for 4% of the time, Pallas kernels for 0%

commit v1 on v0

--- a/solution.py
+++ b/solution.py
@@ -102,7 +102,9 @@
     section_ids = jnp.arange(destination.shape[0], dtype=jnp.int32)
     source = jnp.sum(jnp.where(destination == my_section, section_ids, 0))
     own_projected = adapt_input(block_out, modulation[my_step], down_weight)
-    gathered = lax.all_gather(own_projected, "sec", axis=0, tiled=True)
+    gathered = jnp.concatenate(
+        lax.all_to_all(jnp.stack([own_projected] * lax.axis_size("sec")), "sec", 0, 0), axis=0
+    )
     first_row = jnp.int32(0)
     piece_rows = gathered.shape[0]
     offset = jnp.clip(source, 0, piece_rows - 1)

time: 305 us -> 293 us (0.961)
  blocking collectives: 23.3 us -> 0 us
  waiting for transfers between devices: 94.3 us -> 103 us
    all_gather x1 -> x0, blocking collectives: 23.3 us -> none  [body(): gathered = lax.all_gather(own_projected, 'sec', axis=0, tiled=True)]
    all_to_all x0 -> x1, waiting for transfers between devices: none -> 5.43 us  [body(): lax.all_to_all(jnp.stack([own_projected] * lax.axis_size('sec')), 'sec',...]
    ppermute x1, starting transfers between devices: 9.18 us -> 4.47 us  [extended(): lax.ppermute(lax.slice_in_dim(block, 0, width, axis=dim), axis, backward)]
    all_to_all x0 -> x1, starting transfers between devices: none -> 4.15 us  [body(): lax.all_to_all(jnp.stack([own_projected] * lax.axis_size('sec')), 'sec',...]
    unnamed x23 -> x21, local copies, waits for them, and re-layouts: 16 us -> 16.1 us
  transfers between devices with their start and end apart: 6 -> 7, of which waited for: 5 -> 6; matrix products, arithmetic and copies ran while one was open for 4% -> 5% of each run, Pallas kernels for 0% -> 0%
where the time goes in v1:
time: 293 us; the launch traced here: 291 us
  waiting for transfers between devices  103 us (35%)
  other arithmetic  57.5 us (20%)
  matrix products  45.2 us (15%)
  starting transfers between devices  44.6 us (15%)
  local copies, waits for them, and re-layouts  34.7 us (12%)
  between operations  5.88 us (2%)
    all_to_all x1, waiting for transfers between devices, body(): lax.all_to_all(by_heads(queries), 'ctx', split_axis=2, concat_axis=1, til...  25.9 us
    all_to_all x1, waiting for transfers between devices, body(): lax.all_to_all(by_heads(key_vectors), 'ctx', split_axis=2, concat_axis=1,...  25.9 us
    unnamed x1, other arithmetic  24.4 us
    all_to_all x1, waiting for transfers between devices, body(): lax.all_to_all(local_out, 'ctx', split_axis=1, concat_axis=2, tiled=True)  23.8 us
    dot_general x8, matrix products, one_block(): jnp.einsum('nqhd,nkhd->nhqk', query_block, key_part, preferred_element_ty...  22 us
    all_to_all x1, waiting for transfers between devices, body(): lax.all_to_all(by_heads(value_vectors), 'ctx', split_axis=2, concat_axis=...  20.5 us
    dot_general x8, matrix products, one_block(): jnp.einsum('nhqk,nkhd->nqhd', rounded, value_part, preferred_element_type...  19.4 us
    reduce_sum x8, other arithmetic, one_block(): row_total = jnp.sum(weights, axis=3)  17.3 us
  transfers between devices with their start and end apart: 7, of which 6 were waited for; matrix products, arithmetic and copies ran while one was open for 5% of the time, Pallas kernels for 0%

profile of v1, /device:TPU:1, one launch (start us, length us, event | category | flops | bytes accessed | tf_op | source)
XLA Modules:
  0.0 290.8 jit_solution(4026313118678740126)
XLA Ops:
  2.4 12.8 %all-to-all-start = ((bf16[1,128,32,128]{1,3,0,2:T(8,128)(2,1)}), bf16[1,128,32,128]{1,3,0,2:T(8,128)(2,1)}, u32[]{:S(2)}, u32[]{:S(2)}) async-start(bf16[1,128,32,128]{1,3,0,2:T(8,128)(2,1)} %bitcast.98), calls=%async_computation | async-start | bytes 2097152 | tf_op jit(solution)/shard_map/all_to_all | solution.py:91
  17.5 25.9 %all-to-all-done = bf16[1,128,32,128]{1,3,0,2:T(8,128)(2,1)} async-done(((bf16[1,128,32,128]{1,3,0,2:T(8,128)(2,1)}), bf16[1,128,32,128]{1,3,0,2:T(8,128)(2,1)}, u32[]{:S(2)}, u32[]{:S(2)}) %all-to-all-start) | async-done | bytes 1048608 | tf_op jit(solution)/shard_map/all_to_all | solution.py:91
  43.4 5.8 %all-to-all-start.1 = ((bf16[1,128,32,128]{1,3,0,2:T(8,128)(2,1)}), bf16[1,128,32,128]{1,3,0,2:T(8,128)(2,1)}, u32[]{:S(2)}, u32[]{:S(2)}) async-start(bf16[1,128,32,128]{1,3,0,2:T(8,128)(2,1)} %bitcast.97), calls=%async_computation.1 | async-start | bytes 2097152 | tf_op jit(solution)/shard_map/all_to_all | solution.py:92
  51.6 25.9 %all-to-all-done.1 = bf16[1,128,32,128]{1,3,0,2:T(8,128)(2,1)} async-done(((bf16[1,128,32,128]{1,3,0,2:T(8,128)(2,1)}), bf16[1,128,32,128]{1,3,0,2:T(8,128)(2,1)}, u32[]{:S(2)}, u32[]{:S(2)}) %all-to-all-start.1) | async-done | bytes 1048608 | tf_op jit(solution)/shard_map/all_to_all | solution.py:92
  77.5 5.9 %all-to-all-start.2 = ((bf16[1,128,32,128]{1,3,0,2:T(8,128)(2,1)}), bf16[1,128,32,128]{1,3,0,2:T(8,128)(2,1)}, u32[]{:S(2)}, u32[]{:S(2)}) async-start(bf16[1,128,32,128]{1,3,0,2:T(8,128)(2,1)} %bitcast.96), calls=%async_computation.2 | async-start | bytes 2097152 | tf_op jit(solution)/shard_map/all_to_all | solution.py:93
  91.0 20.5 %all-to-all-done.2 = bf16[1,128,32,128]{1,3,0,2:T(8,128)(2,1)} async-done(((bf16[1,128,32,128]{1,3,0,2:T(8,128)(2,1)}), bf16[1,128,32,128]{1,3,0,2:T(8,128)(2,1)}, u32[]{:S(2)}, u32[]{:S(2)}) %all-to-all-start.2) | async-done | bytes 1048608 | tf_op jit(solution)/shard_map/all_to_all | solution.py:93
  113.8 64.0 %while.11 = (s32[]{:T(128)}, bf16[8,1,512,1,128]{4,2,3,1,0:T(8,128)(2,1)}, bf16[8,1,512,1,128]{4,2,3,1,0:T(8,128)(2,1)}, bf16[1,4096,1,128]{3,1,2,0:T(8,128)(2,1...) while((s32[]{:T(128)}, bf16[8,1,512,1,128]{4,2,3,1,0:T(8,128)(2,1)}, ...), condition=%wide.region_4.5_spmd.clone, body=%wide.region_1.4_spmd.clone.sunk | while | flops 1096977408 | bytes 31746172 | solution.py:51
  114.4 2.7 fusion.69
  122.4 2.7 fusion.69
  130.4 2.7 fusion.69
  146.4 2.7 fusion.69
  154.4 2.7 fusion.69
  170.4 2.7 fusion.69
  177.8 4.3 %copy.55 = bf16[1,4096,1,128]{3,2,0,1:T(2,128)(2,1)} copy(bf16[1,4096,1,128]{3,1,2,0:T(8,128)(2,1)} %bitcast.100) | data formatting | bytes 2097152 | tf_op jit(solution)/shard_map/reshape;transpose | solution.py:52
  182.6 24.4 %reduce.6 = bf16[4096,128]{1,0:T(8,128)(2,1)} reduce(bf16[4096,1,1,128]{3,2,1,0:T(2,128)(2,1)} %bitcast.94, bf16[]{:T(256)} %broadcast.152), dimensions={1,2}, to_apply=%bitcast.82.reduce_sub_computation | reduce | bytes 2097154
  209.2 5.9 %all-to-all-start.3 = ((bf16[32,2,8192]{2,1,0:T(2,128)(2,1)}), bf16[32,2,8192]{2,1,0:T(2,128)(2,1)}, u32[]{:S(2)}, u32[]{:S(2)}) async-start(bf16[32,2,8192]{2,1,0:T(2,128)(2,1)} %reshape.181), calls=%async_computation.3 | async-start | bytes 2097152 | tf_op jit(solution)/shard_map/all_to_all | solution.py:97
  219.3 23.8 %all-to-all-done.3 = bf16[32,2,8192]{2,1,0:T(2,128)(2,1)} async-done(((bf16[32,2,8192]{2,1,0:T(2,128)(2,1)}), bf16[32,2,8192]{2,1,0:T(2,128)(2,1)}, u32[]{:S(2)}, u32[]{:S(2)}) %all-to-all-start.3) | async-done | bytes 1048608 | tf_op jit(solution)/shard_map/all_to_all | solution.py:97
  243.1 5.8 %reshape.182 = bf16[4096,1,1,128]{3,2,1,0:T(2,128)(2,1)} reshape(bf16[32,2,8192]{2,1,0:T(2,128)(2,1)} %all-to-all-done.3) | data formatting | bytes 2097152
  248.8 3.8 %bitcast_convert_fusion = f32[1,4096,1,128]{3,2,0,1:T(1,128)S(1)} fusion(bf16[4096,1,1,128]{3,2,1,0:T(2,128)(2,1)} %reshape.182), kind=kLoop, calls=%fused_computation.65 | loop fusion | flops 524288 | bytes 3145728 | tf_op jit(solution)/shard_map/convert_element_type | solution.py:100
  262.2 4.2 %all-to-all-start.4 = ((bf16[8,1,128,256]{3,2,1,0:T(8,128)(2,1)}), bf16[8,1,128,256]{3,2,1,0:T(8,128)(2,1)}, u32[]{:S(2)}, u32[]{:S(2)}) async-start(bf16[8,1,128,256]{3,2,1,0:T(8,128)(2,1)} %stack.2), calls=%async_computation.4 | async-start | bytes 1048576 | tf_op jit(solution)/shard_map/all_to_all | solution.py:106
  268.9 5.4 %all-to-all-done.4 = bf16[8,1,128,256]{3,2,1,0:T(8,128)(2,1)} async-done(((bf16[8,1,128,256]{3,2,1,0:T(8,128)(2,1)}), bf16[8,1,128,256]{3,2,1,0:T(8,128)(2,1)}, u32[]{:S(2)}, u32[]{:S(2)}) %all-to-all-start.4) | async-done | bytes 524320 | tf_op jit(solution)/shard_map/all_to_all | solution.py:106
  275.5 4.5 %collective-permute-start.1 = (bf16[1,1,8,8,256]{4,0,3,2,1:T(2,128)(2,1)S(1)}, bf16[1,1,8,8,256]{4,0,3,2,1:T(2,128)(2,1)S(1)}, u32[]{:S(2)}, u32[]{:S(2)}) collective-permute-start(bf16[1,1,8,8,256]{4,0,3,2,1:T(2,128)(2,1)S(1)} %get-tuple-element.97), channel_id=1, source_target_pairs={{1,0},{2,1},{3,2},{4,3},{5,4},{6,5},{7,6},{8,7},{9,8},{10,9},{11,1... | collective-permute-start | bytes 98312 | tf_op jit(solution)/shard_map/ppermute | solution.py:20
  280.0 5.6 %collective-permute-start = (bf16[1,1,8,8,256]{4,0,3,2,1:T(2,128)(2,1)S(1)}, bf16[1,1,8,8,256]{4,0,3,2,1:T(2,128)(2,1)S(1)}, u32[]{:S(2)}, u32[]{:S(2)}) collective-permute-start(bf16[1,1,8,8,256]{4,0,3,2,1:T(2,128)(2,1)S(1)} %get-tuple-element.96), channel_id=1, source_target_pairs={{0,1},{1,2},{2,3},{3,4},{4,5},{5,6},{6,7},{7,8},{8,9},{9,10},{10,1... | collective-permute-start | bytes 98312 | tf_op jit(solution)/shard_map/ppermute | solution.py:17
  286.9 3.2 %fusion.42 = bf16[1,2,8,8,256]{4,0,3,2,1:T(2,128)(2,1)S(1)} fusion(bf16[3,3,3,256,256]{4,3,2,1,0:T(8,128)(2,1)S(1)} %copy-done, bf16[1,1,8,8,256]{4,0,3,2,1:T(2,128)(2,1)S(1)} %collective-permute-done.1, bf16[1,2,8,8,256]{4,0,3,2,1:T(2,128)(2,1)S(1)} %broadcast_select_fusion, bf16[1,1,8,8,256]{4,0,3,2,1:T(2,128)(2,1)S(1)} %collective-permute-done, ...), kind=kOutput, calls=%fused_computation.40 | convolution fusion | flops 381157376 | bytes 3735554 | tf_op jit(solution)/shard_map/conv_general_dilated | solution.py:119
  (84 shorter events, 80.7 us)
Async XLA Ops:
  0.0 286.9 %copy-start = (bf16[3,3,3,256,256]{4,3,2,1,0:T(8,128)(2,1)S(1)}, bf16[3,3,3,256,256]{4,3,2,1,0:T(8,128)(2,1)}, u32[]{:S(2)}) copy-start(bf16[3,3,3,256,256]{4,3,2,1,0:T(8,128)(2,1)} %param.18) | copy-start | bytes 10616836
  2.4 41.0 %all-to-all-start = ((bf16[1,128,32,128]{1,3,0,2:T(8,128)(2,1)}), bf16[1,128,32,128]{1,3,0,2:T(8,128)(2,1)}, u32[]{:S(2)}, u32[]{:S(2)}) async-start(bf16[1,128,32,128]{1,3,0,2:T(8,128)(2,1)} %bitcast.98), calls=%async_computation | async-start | bytes 2097152 | tf_op jit(solution)/shard_map/all_to_all | solution.py:91
  43.4 34.0 %all-to-all-start.1 = ((bf16[1,128,32,128]{1,3,0,2:T(8,128)(2,1)}), bf16[1,128,32,128]{1,3,0,2:T(8,128)(2,1)}, u32[]{:S(2)}, u32[]{:S(2)}) async-start(bf16[1,128,32,128]{1,3,0,2:T(8,128)(2,1)} %bitcast.97), calls=%async_computation.1 | async-start | bytes 2097152 | tf_op jit(solution)/shard_map/all_to_all | solution.py:92
  49.3 34.0 %copy-start.6 = (s32[8]{0:T(128)S(1)}, s32[8]{0:T(128)}, u32[]{:S(2)}) copy-start(s32[8]{0:T(128)} %param.20) | copy-start | bytes 100
  49.3 36.6 %copy-start.4 = (s32[8]{0:T(128)S(1)}, s32[8]{0:T(128)}, u32[]{:S(2)}) copy-start(s32[8]{0:T(128)} %param.19) | copy-start | bytes 100
  77.5 34.0 %all-to-all-start.2 = ((bf16[1,128,32,128]{1,3,0,2:T(8,128)(2,1)}), bf16[1,128,32,128]{1,3,0,2:T(8,128)(2,1)}, u32[]{:S(2)}, u32[]{:S(2)}) async-start(bf16[1,128,32,128]{1,3,0,2:T(8,128)(2,1)} %bitcast.96), calls=%async_computation.2 | async-start | bytes 2097152 | tf_op jit(solution)/shard_map/all_to_all | solution.py:93
  117.2 2.2 copy-start.1
  125.2 2.2 copy-start.1
  133.2 2.2 copy-start.1
  141.2 2.2 copy-start.1
  149.2 2.2 copy-start.1
  157.2 2.2 copy-start.1
  165.2 2.2 copy-start.1
  173.2 2.2 copy-start.1
  207.0 8.0 %copy-start.7 = (s32[8]{0:T(128)S(1)}, s32[8]{0:T(128)}, u32[]{:S(2)}) copy-start(s32[8]{0:T(128)} %param.21) | copy-start | bytes 100
  209.2 33.9 %all-to-all-start.3 = ((bf16[32,2,8192]{2,1,0:T(2,128)(2,1)}), bf16[32,2,8192]{2,1,0:T(2,128)(2,1)}, u32[]{:S(2)}, u32[]{:S(2)}) async-start(bf16[32,2,8192]{2,1,0:T(2,128)(2,1)} %reshape.181), calls=%async_computation.3 | async-start | bytes 2097152 | tf_op jit(solution)/shard_map/all_to_all | solution.py:97
  257.9 2.9 copy-start.2
  257.9 2.9 copy-start.3
  257.9 2.9 copy-start.5
  262.2 12.1 %all-to-all-start.4 = ((bf16[8,1,128,256]{3,2,1,0:T(8,128)(2,1)}), bf16[8,1,128,256]{3,2,1,0:T(8,128)(2,1)}, u32[]{:S(2)}, u32[]{:S(2)}) async-start(bf16[8,1,128,256]{3,2,1,0:T(8,128)(2,1)} %stack.2), calls=%async_computation.4 | async-start | bytes 1048576 | tf_op jit(solution)/shard_map/all_to_all | solution.py:106
  275.5 10.1 %collective-permute-start.1 = (bf16[1,1,8,8,256]{4,0,3,2,1:T(2,128)(2,1)S(1)}, bf16[1,1,8,8,256]{4,0,3,2,1:T(2,128)(2,1)S(1)}, u32[]{:S(2)}, u32[]{:S(2)}) collective-permute-start(bf16[1,1,8,8,256]{4,0,3,2,1:T(2,128)(2,1)S(1)} %get-tuple-element.97), channel_id=1, source_target_pairs={{1,0},{2,1},{3,2},{4,3},{5,4},{6,5},{7,6},{8,7},{9,8},{10,9},{11,1... | collective-permute-start | bytes 98312 | tf_op jit(solution)/shard_map/ppermute | solution.py:20
  280.0 6.9 %collective-permute-start = (bf16[1,1,8,8,256]{4,0,3,2,1:T(2,128)(2,1)S(1)}, bf16[1,1,8,8,256]{4,0,3,2,1:T(2,128)(2,1)S(1)}, u32[]{:S(2)}, u32[]{:S(2)}) collective-permute-start(bf16[1,1,8,8,256]{4,0,3,2,1:T(2,128)(2,1)S(1)} %get-tuple-element.96), channel_id=1, source_target_pairs={{0,1},{1,2},{2,3},{3,4},{4,5},{5,6},{6,7},{7,8},{8,9},{9,10},{10,1... | collective-permute-start | bytes 98312 | tf_op jit(solution)/shard_map/ppermute | solution.py:17
